TPU v7x, 128 devices: a whole 4x4x4 slice. The times are simulated.
128 devices in a mesh: replica: 8 (over z, core), fsdp: 16 (over y, x).
Axes of the slice: x: 4, y: 4, z: 4, core: 2. Of those that a mesh axis runs over, the one named last changes fastest.
Arguments:
- outer_grad: bfloat16 [8, 4096, 14336], P('replica', 'fsdp'), may hold values from -64 to 64
- error_prev: bfloat16 [8, 4096, 14336], P('replica', 'fsdp'), may hold values from -6 to 6
- q_init: float32 [8, 14336], replicated, may hold values from -6 to 6
Outputs:
- update: bfloat16 [4096, 14336], P('fsdp', 'replica')
- new_error: bfloat16 [8, 4096, 14336], P('replica', 'fsdp')
All inputs are finite; a program needn't handle non-finite values.
Results may differ from a plain program's by a relative error of at most 0.0011.
Values sent between devices are 32-bit elements; how exact they have to be, the bound alone decides.
A program may use at most 128 MiB of HBM per device.

v0:
```python
import jax
import jax.numpy as jnp
from jax import lax
from jax.sharding import PartitionSpec as P

HIGHEST = lax.Precision.HIGHEST


def contract_rows(left, right):
    return lax.dot_general(left, right, (((0,), (0,)), ((), ())), precision=HIGHEST)


def project(merged, factor):
    return lax.dot_general(merged, factor, (((1,), (1,)), ((), ())), precision=HIGHEST)


def cholesky_left(gram, image):
    lower = jnp.linalg.cholesky(gram)
    solved = lax.linalg.triangular_solve(lower, image.T, left_side=True, lower=True)
    return (lower, solved.T)


def refine(merged, image):
    gram = lax.psum(contract_rows(image, image), "fsdp")
    lower, left_rows = cholesky_left(gram, image)
    factor = lax.psum(contract_rows(left_rows, merged), "fsdp")
    return (left_rows, factor)


def shards(outer_grad, error_prev, q_init):
    merged = outer_grad[0].astype(jnp.float32) + error_prev[0].astype(jnp.float32)
    replicas = lax.axis_size("replica")
    factor = q_init
    left_rows, factor = refine(merged, project(merged, factor))
    image = project(merged, factor)
    left_rows, factor = refine(merged, image)
    rows_all, factors_all = (
        lax.all_gather(left_rows[None], "replica", axis=0, tiled=True),
        lax.all_gather(factor[None], "replica", axis=0, tiled=True),
    )
    approx = jnp.dot(left_rows, factor, precision=HIGHEST)
    new_error = (merged - approx).astype(jnp.bfloat16)[None]
    local_rows = merged.shape[0]
    rank_count = left_rows.shape[1]
    width_piece = merged.shape[1] // replicas
    start_col = lax.axis_index("replica") * width_piece
    stacked_rows = jnp.transpose(rows_all, (1, 0, 2)).reshape(local_rows, replicas * rank_count)
    stacked_factors = factors_all.reshape(replicas * rank_count, merged.shape[1])
    column_block = lax.dynamic_slice_in_dim(stacked_factors, start_col, width_piece, 1)
    update = (jnp.dot(stacked_rows, column_block, precision=HIGHEST) / replicas).astype(
        jnp.bfloat16
    )
    return (update, new_error)


def solution(mesh):
    return jax.shard_map(
        shards,
        mesh=mesh,
        in_specs=(P("replica", "fsdp", None), P("replica", "fsdp", None), P()),
        out_specs=(P("fsdp", "replica"), P("replica", "fsdp", None)),
        check_vma=False,
    )
```

profile of v0, /device:TPU:17, one launch (start us, length us, event | category | flops | bytes accessed | tf_op | source)
XLA Modules:
  0.0 352.0 jit_solution(14151113251271086866)
XLA Ops:
  7.2 0.0 copy-start
  7.2 0.0 all-reduce.3.cloned.1.call-start
  7.2 1.0 copy-done
  8.2 15.2 %fusion.8 = f32[256,8]{0,1:T(8,128)S(1)} fusion(f32[8,14336]{1,0:T(8,128)S(1)} %copy-done, bf16[1,256,14336]{2,1,0:T(8,128)(2,1)} %param.7, bf16[1,256,14336]{2,1,0:T(8,128)(2,1)} %param.6), kind=kOutput, calls=%fused_computation.9 | convolution fusion | flops 363331584 | bytes 15147008 | tf_op jit(solution)/shard_map/dot_general | solution.py:14
  23.4 0.1 fusion.25
  23.5 26.2 %psum.28 = f32[8,8]{0,1:T(8,128)S(1)} all-reduce(f32[8,8]{0,1:T(8,128)S(1)} %fusion.25), channel_id=1, replica_groups=mesh['replica'=8,'fsdp'=16] {'fsdp'}, use_global_device_ids=true, to_apply=%region_0.0 | all-reduce | flops 64 | bytes 512 | tf_op jit(solution)/shard_map/psum | solution.py:24
  49.8 0.1 copy.6
  49.9 0.7 cholesky.44
  50.6 0.6 compare_reduce_fusion.1
  51.3 0.6 fusion.16
  51.9 0.6 custom-call.6
  52.5 0.2 fusion.14
  52.7 12.1 %fusion.6 = f32[8,14336]{1,0:T(8,128)} fusion(f32[8,256]{1,0:T(8,128)S(1)} %fusion.14, bf16[1,256,14336]{2,1,0:T(8,128)(2,1)} %param.7, bf16[1,256,14336]{2,1,0:T(8,128)(2,1)} %param.6), kind=kOutput, calls=%fused_computation.7 | convolution fusion | flops 363331584 | bytes 15147008 | tf_op jit(solution)/shard_map/dot_general | solution.py:10
  64.9 0.0 all-reduce.3.cloned.1.call-update
  64.9 0.2 all-reduce.5.cloned.1.call-start
  65.1 92.8 %all-reduce.3.cloned.1.call-done = f32[8,14336]{1,0:T(8,128)} async-done(((f32[8,14336]{1,0:T(8,128)}), f32[8,14336]{1,0:T(8,128)}) %all-reduce.3.cloned.1.call-update) | async-done | bytes 458768 | tf_op jit(solution)/shard_map/psum | solution.py:26
  157.9 15.2 %fusion.4 = f32[256,8]{0,1:T(8,128)S(1)} fusion(f32[8,14336]{1,0:T(8,128)} %all-reduce.3.cloned.1.call-done, bf16[1,256,14336]{2,1,0:T(8,128)(2,1)} %param.7, bf16[1,256,14336]{2,1,0:T(8,128)(2,1)} %param.6), kind=kOutput, calls=%fused_computation.5 | convolution fusion | flops 363331584 | bytes 15147008 | tf_op jit(solution)/shard_map/dot_general | solution.py:14
  173.1 0.1 fusion.26
  173.3 25.7 %psum.30 = f32[8,8]{0,1:T(8,128)S(1)} all-reduce(f32[8,8]{0,1:T(8,128)S(1)} %fusion.26), channel_id=1, replica_groups=mesh['replica'=8,'fsdp'=16] {'fsdp'}, use_global_device_ids=true, to_apply=%region_4.7 | all-reduce | flops 64 | bytes 512 | tf_op jit(solution)/shard_map/psum | solution.py:24
  199.0 0.1 copy.9
  199.1 0.7 cholesky.55
  199.8 0.6 compare_reduce_fusion
  200.5 0.6 fusion.17
  201.1 0.6 custom-call.7
  201.8 0.2 fusion.12
  202.0 12.1 %fusion.2 = f32[8,14336]{1,0:T(8,128)} fusion(f32[8,256]{1,0:T(8,128)S(1)} %fusion.12, bf16[1,256,14336]{2,1,0:T(8,128)(2,1)} %param.7, bf16[1,256,14336]{2,1,0:T(8,128)(2,1)} %param.6), kind=kOutput, calls=%fused_computation.3 | convolution fusion | flops 363331584 | bytes 15147008 | tf_op jit(solution)/shard_map/dot_general | solution.py:10
  214.1 0.0 all-reduce.5.cloned.1.call-update
  214.1 0.0 all-gather.4.cloned.1.call-start
  214.2 93.2 %all-reduce.5.cloned.1.call-done = f32[8,14336]{1,0:T(8,128)} async-done(((f32[8,14336]{1,0:T(8,128)}), f32[8,14336]{1,0:T(8,128)}) %all-reduce.5.cloned.1.call-update) | async-done | bytes 458768 | tf_op jit(solution)/shard_map/psum | solution.py:26
  307.4 0.0 all-gather.4.cloned.1.call-update
  307.4 15.6 %all-gather = f32[2048,8]{0,1:T(8,128)S(1)} all-gather(f32[256,8]{0,1:T(8,128)S(1)} %bitcast.56), channel_id=2, replica_groups=mesh['replica'=8,'fsdp'=16] {'replica'}, dimensions={0}, use_global_device_ids=true | all-gather | bytes 73728 | tf_op jit(solution)/shard_map/all_gather | solution.py:38
  323.0 18.3 %fusion.1 = bf16[1,256,14336]{2,1,0:T(8,128)(2,1)} fusion(f32[8,256]{1,0:T(8,128)S(1)} %fusion.12, f32[8,14336]{1,0:T(8,128)} %all-reduce.5.cloned.1.call-done, bf16[1,256,14336]{2,1,0:T(8,128)(2,1)} %param.7, bf16[1,256,14336]{2,1,0:T(8,128)(2,1)} %param.6), kind=kOutput, calls=%fused_computation.2 | convolution fusion | flops 370671616 | bytes 22487040 | tf_op jit(solution)/shard_map/dot_general | solution.py:41
  341.2 0.7 all-gather.4.cloned.1.call-done
  341.9 3.6 %fusion.10 = bf16[256,1792]{1,0:T(8,128)(2,1)} fusion(f32[256,64]{0,1:T(8,128)S(1)} %bitcast.55, f32[64,14336]{1,0:T(8,128)} %all-gather.4.cloned.1.call-done, s32[]{:T(128)S(6)} %select_n.6), kind=kOutput, calls=%fused_computation.13 | convolution fusion | flops 353239040 | bytes 1441796 | tf_op jit(solution)/shard_map/dot_general | solution.py:50
  (4 shorter events, 0.1 us)
Async XLA Ops:
  7.2 1.0 copy-start
  7.2 150.7 %all-reduce.3.cloned.1.call-start = ((), (), s32[]{:S(2)}) async-start(), calls=%async_computation | async-start | bytes 917504 | tf_op jit(solution)/shard_map/psum | solution.py:26
  64.9 242.5 %all-reduce.5.cloned.1.call-start = ((), (), s32[]{:S(2)}) async-start(), calls=%async_computation.1 | async-start | bytes 917504 | tf_op jit(solution)/shard_map/psum | solution.py:26
  214.1 127.8 %all-gather.4.cloned.1.call-start = ((), (), s32[]{:S(2)}) async-start(), calls=%async_computation.2 | async-start | bytes 4128768 | tf_op jit(solution)/shard_map/all_gather | solution.py:39
Sparse Core Ops, SparseCore 0:
  65.0 92.8 all-reduce.2
  214.2 93.0 all-reduce.4
  309.0 32.8 all-gather.3
where the time goes:
time: 354 us; the launch traced here: 352 us
  waiting for transfers between devices  187 us (53%)
  matrix products  77.2 us (22%)
  blocking collectives  67.6 us (19%)
  between operations  13.8 us (4%)
  other arithmetic  5.35 us (2%)
    psum x2, waiting for transfers between devices, refine(): factor = lax.psum(contract_rows(left_rows, merged), 'fsdp')  186 us
    psum x2, blocking collectives, refine(): gram = lax.psum(contract_rows(image, image), 'fsdp')  52 us
    dot_general x2, matrix products, project(): lax.dot_general(merged, factor, (((1,), (1,)), ((), ())), precision=HIGHEST)  30.4 us
    dot_general x4, matrix products, contract_rows(): lax.dot_general(left, right, (((0,), (0,)), ((), ())), precision=HIGHEST)  24.6 us
    dot_general x1, matrix products, shards(): approx = jnp.dot(left_rows, factor, precision=HIGHEST)  18.3 us
    all_gather x1, blocking collectives, shards(): lax.all_gather(left_rows[None], 'replica', axis=0, tiled=True)  15.6 us
  transfers between devices with their start and end apart: 3, of which 3 were waited for; matrix products, arithmetic and copies ran while one was open for 5% of the time, Pallas kernels for 0%

commit v1 on v0

v1 whole, which is shorter than its diff:
```python
import functools

import jax
import jax.numpy as jnp
from jax import lax
from jax.experimental import pallas as pl
from jax.experimental.pallas import tpu as pltpu
from jax.sharding import PartitionSpec as P

F32, BF16 = jnp.float32, jnp.bfloat16
NT = (((1,), (1,)), ((), ()))
MESH = pl.DeviceIdType.MESH


def dot(a, b):
    return jnp.dot(a, b, preferred_element_type=F32)


def dot_nt(a, b, **kw):
    return lax.dot_general(a, b, NT, preferred_element_type=F32, **kw)


def pieces(x):
    hi = x.astype(BF16).astype(F32)
    rest = x - hi
    mid = rest.astype(BF16).astype(F32)
    return jnp.concatenate([hi, mid, rest - mid, jnp.zeros_like(x)], axis=0).astype(BF16)


def fold(x, rank):
    return x[:rank] + x[rank : 2 * rank] + x[2 * rank : 3 * rank]


def inverse_cholesky(gram, rank):
    row = lax.broadcasted_iota(jnp.int32, gram.shape, 0)
    lane = lax.broadcasted_iota(jnp.int32, gram.shape, 1)
    aug = jnp.where(lane < rank, gram, jnp.where(lane == row + rank, 1.0, 0.0))
    for k in range(rank):
        scale = lax.rsqrt(aug[k : k + 1, k : k + 1])
        pivot = aug[k : k + 1, :] * scale
        below = aug - (aug[:, k : k + 1] * scale) * pivot
        aug = jnp.where(row == k, pivot, jnp.where(row > k, below, aug))
    return aug


def apply_inverse(aug, x, rank):
    out = aug[:, rank : rank + 1] * x[0:1]
    for k in range(1, rank):
        out += aug[:, rank + k : rank + k + 1] * x[k : k + 1]
    return out


def kernel(
    n_rep, n_fsdp, side, g_hbm, e_hbm, q_hbm, ne_ref, up_ref,
    g, e, q, img, gram_in, s_out, s_in, f_own, f_all, z_rows, z_fac,
    load_sem, gram_send, gram_recv, s_send, s_recv, f_send, f_recv, zr_send, zr_recv, zf_send, zf_recv,
):
    rank, cols = q.shape
    piece = cols // n_fsdp
    pairs, pair = n_fsdp // 2, 2 * piece
    rep, me = lax.axis_index("replica"), lax.axis_index("fsdp")
    my_y, my_x = me // side, me % side

    barrier = pltpu.get_barrier_semaphore()
    for t in range(1, n_fsdp):
        pl.semaphore_signal(barrier, inc=1, device_id={"fsdp": lax.rem(me + t, n_fsdp)}, device_id_type=MESH)
    for t in range(1, n_rep):
        pl.semaphore_signal(barrier, inc=1, device_id={"replica": lax.rem(rep + t, n_rep)}, device_id_type=MESH)

    loads = [pltpu.make_async_copy(q_hbm, q, load_sem.at[0])]
    for c in range(pairs):
        at = pl.ds(c * pair, pair)
        loads.append(pltpu.make_async_copy(g_hbm.at[0, :, at], g.at[:, at], load_sem.at[1 + 2 * c]))
        loads.append(pltpu.make_async_copy(e_hbm.at[0, :, at], e.at[:, at], load_sem.at[2 + 2 * c]))
    for copy in loads:
        copy.start()

    def others():
        steps = [(dy, dx) for dy in range(side) for dx in range(side) if dy or dx]
        steps.sort(key=lambda s: -(min(s[0], side - s[0]) + min(s[1], side - s[1])))
        return [lax.rem(my_y + dy, side) * side + lax.rem(my_x + dx, side) for dy, dx in steps]

    def to_peer(src, dst, send, recv, peer):
        return pltpu.make_async_remote_copy(
            src_ref=src, dst_ref=dst, send_sem=send, recv_sem=recv, device_id={"fsdp": peer}, device_id_type=MESH
        )

    def gram_copy(it, peer, slot):
        return to_peer(
            gram_in.at[it, me], gram_in.at[it, slot], gram_send.at[it, peer], gram_recv.at[it, slot], peer
        )

    def s_copy(it, peer, slot):
        return to_peer(s_out.at[it, peer], s_in.at[it, slot], s_send.at[it, peer], s_recv.at[it, slot], peer)

    def f_copy(it, peer, slot):
        return to_peer(f_own.at[it], f_all.at[it, slot], f_send.at[it, peer], f_recv.at[it, slot], peer)

    def f_local(it):
        return pltpu.make_async_copy(f_own.at[it], f_all.at[it, me], f_recv.at[it, me])

    def f_pair(it, pp):
        for k in range(2):
            pltpu.make_async_copy(f_own.at[it], f_all.at[it, 2 * pp + k], f_recv.at[it, 2 * pp + k]).wait()
        return jnp.concatenate([f_all[it, 2 * pp], f_all[it, 2 * pp + 1]], axis=1)

    def columns(pp):
        return pl.ds(pl.multiple_of(pp * pair, pair), pair)

    def sweep(it, image):
        wide = jnp.concatenate([image, jnp.zeros((128 - rank, image.shape[1]), F32)], axis=0)
        gram_in[it, me] = dot_nt(image, wide, precision=lax.Precision.HIGHEST)
        for peer in others():
            gram_copy(it, peer, me).start()
        left = pieces(image)
        mine = me // 2
        for t in list(range(1, pairs)) + [0]:
            pp = lax.rem(mine + t, pairs)
            at = columns(pp)
            part = fold(dot(left, g[:, at]) + dot(left, e[:, at]), rank)
            s_out[it, 2 * pp] = part[:, :piece]
            s_out[it, 2 * pp + 1] = part[:, piece:]
            if t:
                s_copy(it, 2 * pp, me).start()
                s_copy(it, 2 * pp + 1, me).start()
            else:
                s_copy(it, me + 1 - 2 * lax.rem(me, 2), me).start()
        for peer in others():
            gram_copy(it, peer, peer).wait_recv()
        gram = gram_in[it, 0]
        for p in range(1, n_fsdp):
            gram += gram_in[it, p]
        inv = inverse_cholesky(gram, rank)
        total = s_out[it, me]
        for peer in others()[::-1]:
            s_copy(it, peer, peer).wait_recv()
            total += s_in[it, peer]
        f_own[it] = apply_inverse(inv, total, rank)
        for peer in others():
            f_copy(it, peer, me).start()
        f_local(it).start()
        return inv

    loads[0].wait()
    image = jnp.zeros((4 * rank, g.shape[0]), F32)
    for c in range(pairs):
        at = pl.ds(c * pair, pair)
        start = pieces(q[:, at])
        loads[1 + 2 * c].wait()
        image += dot_nt(start, g[:, at])
        loads[2 + 2 * c].wait()
        image += dot_nt(start, e[:, at])
    pl.semaphore_wait(barrier, n_fsdp + n_rep - 2)
    sweep(0, fold(image, rank))

    image = jnp.zeros((4 * rank, g.shape[0]), F32)
    mine = me // 2
    for t in range(pairs):
        pp = lax.rem(mine + t, pairs)
        factor = pieces(f_pair(0, pp))
        at = columns(pp)
        image += dot_nt(factor, g[:, at])
        image += dot_nt(factor, e[:, at])
    img[...] = fold(image, rank)
    inv = sweep(1, img[...])

    def to_replica(src, dst, send, recv, peer):
        return pltpu.make_async_remote_copy(
            src_ref=src, dst_ref=dst, send_sem=send, recv_sem=recv, device_id={"replica": peer}, device_id_type=MESH
        )

    def row_copy(peer, slot):
        return to_replica(z_rows.at[rep], z_rows.at[slot], zr_send.at[peer], zr_recv.at[slot], peer)

    def factor_copy(peer, slot):
        return to_replica(
            f_all.at[1, pl.ds(2 * peer, 2)], z_fac.at[slot], zf_send.at[peer], zf_recv.at[slot], peer
        )

    rows_t = apply_inverse(inv, img[...], rank)
    z_rows[rep] = rows_t
    replicas = [lax.rem(rep + t, n_rep) for t in range(1, n_rep)]
    for peer in replicas:
        row_copy(peer, rep).start()

    def halves(x):
        hi = x.astype(BF16).astype(F32)
        return hi, x - hi

    hi, mid = halves(rows_t)
    left = jnp.concatenate([hi, hi, mid, mid], axis=0).T.astype(BF16)
    for t in list(range(1, n_rep)) + [0]:
        pp = lax.rem(rep + t, n_rep)
        factor = f_pair(1, pp)
        if t:
            factor_copy(pp, rep).start()
        else:
            z_fac[rep] = f_all[1, pl.ds(2 * rep, 2)]
        hi, mid = halves(factor)
        right = jnp.concatenate([hi, mid, hi, mid], axis=0).astype(BF16)
        at = columns(pp)
        ne_ref[0, :, at] = (g[:, at].astype(F32) + e[:, at].astype(F32) - dot(left, right)).astype(BF16)

    for peer in replicas:
        row_copy(peer, peer).wait_recv()
        factor_copy(peer, peer).wait_recv()
    hi, mid = halves(z_rows[...].reshape(n_rep * rank, -1))
    left = jnp.concatenate([hi, hi, mid], axis=0).T.astype(BF16)
    for k in range(2):
        hi, mid = halves(z_fac[:, k].reshape(n_rep * rank, piece))
        right = jnp.concatenate([hi, mid, hi], axis=0).astype(BF16)
        up_ref[:, k * piece : (k + 1) * piece] = (dot(left, right) * (1.0 / n_rep)).astype(BF16)

    for it in range(2):
        for peer in others():
            gram_copy(it, peer, me).wait_send()
            s_copy(it, peer, me).wait_send()
            f_copy(it, peer, me).wait_send()
    for peer in replicas:
        row_copy(peer, rep).wait_send()
        factor_copy(peer, rep).wait_send()


def shards(n_rep, n_fsdp, outer_grad, error_prev, q_init):
    rank, cols = q_init.shape
    rows = outer_grad.shape[1]
    piece = cols // n_fsdp
    side = 4
    dma = pltpu.SemaphoreType.DMA
    update, new_error = None, None
    new_error, update = pl.pallas_call(
        functools.partial(kernel, n_rep, n_fsdp, side),
        out_shape=OUT((1, rows, cols), (rows, cols // n_rep)),
        in_specs=[pl.BlockSpec(memory_space=pl.ANY)] * 3,
        out_specs=OUT_SPECS,
        scratch_shapes=[
            pltpu.VMEM((rows, cols), BF16),
            pltpu.VMEM((rows, cols), BF16),
            pltpu.VMEM((rank, cols), F32),
            pltpu.VMEM((rank, rows), F32),
            pltpu.VMEM((2, n_fsdp, rank, 128), F32),
            pltpu.VMEM((2, n_fsdp, rank, piece), F32),
            pltpu.VMEM((2, n_fsdp, rank, piece), F32),
            pltpu.VMEM((2, rank, piece), F32),
            pltpu.VMEM((2, n_fsdp, rank, piece), F32),
            pltpu.VMEM((n_rep, rank, rows), F32),
            pltpu.VMEM((n_rep, 2, rank, piece), F32),
            dma((1 + n_fsdp,)),
            dma((2, n_fsdp)),
            dma((2, n_fsdp)),
            dma((2, n_fsdp)),
            dma((2, n_fsdp)),
            dma((2, n_fsdp)),
            dma((2, n_fsdp)),
            dma((n_rep,)),
            dma((n_rep,)),
            dma((n_rep,)),
            dma((n_rep,)),
        ],
        compiler_params=pltpu.CompilerParams(
            collective_id=0, has_side_effects=True, vmem_limit_bytes=VMEM_LIMIT
        ),
    )(outer_grad, error_prev, q_init)
    return update, new_error


VMEM_LIMIT = 40 << 20
OUT_SPECS = [pl.BlockSpec(memory_space=pltpu.VMEM)] * 2


def OUT(a, b):
    return [pltpu.VMEM(a, BF16), pltpu.VMEM(b, BF16)]


def solution(mesh):
    n_rep, n_fsdp = mesh.shape["replica"], mesh.shape["fsdp"]
    return jax.shard_map(
        functools.partial(shards, n_rep, n_fsdp),
        mesh=mesh,
        in_specs=(P("replica", "fsdp", None), P("replica", "fsdp", None), P()),
        out_specs=(P("fsdp", "replica"), P("replica", "fsdp", None)),
        check_vma=False,
    )
```

time: 354 us -> 73.5 us (0.21)
  the two profiles are of different devices: /device:TPU:17 before, /device:TPU:1 now
where the time goes in v1:
time: 73.5 us; the launch traced here: 73.4 us
  Pallas kernels  67.7 us (92%)
  local copies, waits for them, and re-layouts  4.98 us (7%)
    pallas_call x1, Pallas kernels, shards(): pl.pallas_call(functools.partial(kernel, n_rep, n_fsdp, side), out_shape=...  67.7 us
    unnamed x4, local copies, waits for them, and re-layouts  4.98 us

profile of v1, /device:TPU:1, one launch (start us, length us, event | category | flops | bytes accessed | tf_op | source)
XLA Modules:
  0.0 73.4 jit_solution(12061755320613727037)
XLA Ops:
  0.6 0.0 copy-start
  0.6 1.0 %copy-done = f32[8,14336]{1,0:T(8,128)S(1)} copy-done((f32[8,14336]{1,0:T(8,128)S(1)}, f32[8,14336]{1,0:T(8,128)}, u32[]{:S(2)}) %copy-start) | copy-done | bytes 458776
  1.6 67.7 %shard_map.50 = (bf16[1,256,14336]{2,1,0:T(8,128)(2,1)S(1)}, bf16[256,1792]{1,0:T(8,128)(2,1)S(1)}) custom-call(bf16[1,256,14336]{2,1,0:T(8,128)(2,1)} %g_hbm.1, bf16[1,256,14336]{2,1,0:T(8,128)(2,1)} %e_hbm.1, f32[8,14336]{1,0:T(8,128)S(1)} %copy-done), custom_call_target="tpu_custom_call" | custom-call | tf_op jit(solution)/shard_map/pallas_call | solution.py:231
  69.4 0.9 %copy.7 = bf16[256,1792]{1,0:T(8,128)(2,1)} copy(bf16[256,1792]{1,0:T(8,128)(2,1)S(1)} %get-tuple-element.6) | data formatting | bytes 1835008
  70.3 3.0 %copy.8 = bf16[1,256,14336]{2,1,0:T(8,128)(2,1)} copy(bf16[1,256,14336]{2,1,0:T(8,128)(2,1)S(1)} %get-tuple-element.7) | data formatting | bytes 14680064
Async XLA Ops:
  0.6 1.0 %copy-start = (f32[8,14336]{1,0:T(8,128)S(1)}, f32[8,14336]{1,0:T(8,128)}, u32[]{:S(2)}) copy-start(f32[8,14336]{1,0:T(8,128)} %q_hbm.1) | copy-start | bytes 1376260

commit v2 on v1

v2 whole, which is shorter than its diff:
```python
import functools
import math

import jax
import jax.numpy as jnp
from jax import lax
from jax.experimental import pallas as pl
from jax.experimental.pallas import tpu as pltpu
from jax.sharding import PartitionSpec as P

F32, BF16 = jnp.float32, jnp.bfloat16
NT = (((1,), (1,)), ((), ()))
MESH = pl.DeviceIdType.MESH


def dot(a, b):
    return jnp.dot(a, b, preferred_element_type=F32)


def dot_nt(a, b, **kw):
    return lax.dot_general(a, b, NT, preferred_element_type=F32, **kw)


def pieces(x):
    hi = x.astype(BF16).astype(F32)
    rest = x - hi
    mid = rest.astype(BF16).astype(F32)
    return jnp.concatenate([hi, mid, rest - mid, jnp.zeros_like(x)], axis=0).astype(BF16)


def fold(x, rank):
    return x[:rank] + x[rank : 2 * rank] + x[2 * rank : 3 * rank]


def inverse_cholesky(gram, rank):
    row = lax.broadcasted_iota(jnp.int32, gram.shape, 0)
    lane = lax.broadcasted_iota(jnp.int32, gram.shape, 1)

    def step(k, aug):
        top = jnp.sum(jnp.where(row == k, aug, 0.0), axis=0, keepdims=True)
        side = jnp.sum(jnp.where(lane == k, aug, 0.0), axis=1, keepdims=True)
        scale = lax.rsqrt(jnp.sum(jnp.where(row == k, side, 0.0), axis=0, keepdims=True))
        pivot = top * scale
        return jnp.where(row == k, pivot, jnp.where(row > k, aug - (side * scale) * pivot, aug))

    aug = jnp.where(lane < rank, gram, jnp.where(lane == row + rank, 1.0, 0.0))
    return lax.fori_loop(0, rank, step, aug)


def apply_inverse(aug, x, rank):
    out = aug[:, rank : rank + 1] * x[0:1]
    for k in range(1, rank):
        out += aug[:, rank + k : rank + k + 1] * x[k : k + 1]
    return out


def halves(x):
    hi = x.astype(BF16).astype(F32)
    return hi, x - hi


def kernel(
    n_rep, n_fsdp, side, g_hbm, e_hbm, q_hbm, ne_ref, z_rows, z_fac,
    g, e, q, img, inv, gram_in, s_out, s_in, f_own, f_all,
    load_sem, gram_send, gram_recv, s_send, s_recv, f_send, f_recv, zr_send, zr_recv, zf_send, zf_recv,
):
    rank, cols = q.shape
    piece = cols // n_fsdp
    pairs, pair = n_fsdp // 2, 2 * piece
    rep, me = lax.axis_index("replica"), lax.axis_index("fsdp")
    my_y, my_x = me // side, me % side

    def columns(pp):
        return pl.ds(pl.multiple_of(pp * pair, pair), pair)

    def loads(c):
        at = columns(c)
        return (
            pltpu.make_async_copy(g_hbm.at[0, :, at], g.at[:, at], load_sem.at[2 * c]),
            pltpu.make_async_copy(e_hbm.at[0, :, at], e.at[:, at], load_sem.at[2 * c + 1]),
        )

    load_q = pltpu.make_async_copy(q_hbm, q, load_sem.at[2 * pairs])
    load_q.start()
    for c in range(pairs):
        for copy in loads(c):
            copy.start()

    barrier = pltpu.get_barrier_semaphore()
    for t in range(1, n_fsdp):
        pl.semaphore_signal(barrier, inc=1, device_id={"fsdp": lax.rem(me + t, n_fsdp)}, device_id_type=MESH)
    for t in range(1, n_rep):
        pl.semaphore_signal(barrier, inc=1, device_id={"replica": lax.rem(rep + t, n_rep)}, device_id_type=MESH)

    def far(step, size):
        return min(step, size - step)

    def others():
        steps = [(dy, dx) for dy in range(side) for dx in range(side) if dy or dx]
        steps.sort(key=lambda s: far(s[0], side) + far(s[1], side))
        return [lax.rem(my_y + dy, side) * side + lax.rem(my_x + dx, side) for dy, dx in steps]

    def near_pair(t):
        half = side // 2
        u = t // half
        dy = (u + 1) // 2 * (2 * (u % 2) - 1) + side
        return lax.rem(my_y + dy, side) * half + lax.rem(my_x // 2 + t, half)

    def to_peer(src, dst, send, recv, peer):
        return pltpu.make_async_remote_copy(
            src_ref=src, dst_ref=dst, send_sem=send, recv_sem=recv, device_id={"fsdp": peer}, device_id_type=MESH
        )

    def gram_copy(it, peer):
        return to_peer(gram_in.at[it, me], gram_in.at[it, me], gram_send.at[it], gram_recv.at[it], peer)

    def s_copy(it, peer):
        return to_peer(s_out.at[it, peer], s_in.at[it, me], s_send.at[it], s_recv.at[it], peer)

    def f_copy(it, peer):
        return to_peer(f_own.at[it], f_all.at[it, me], f_send.at[it], f_recv.at[it, me // 2], peer)

    def f_local(it):
        return pltpu.make_async_copy(f_own.at[it], f_all.at[it, me], f_recv.at[it, me // 2])

    def from_others(buffer, sem):
        part = buffer.at[pl.ds(0, buffer.shape[0] - 1)]
        return pltpu.make_async_copy(part, part, sem)

    def f_pair(it, pp):
        both = f_all.at[it, pl.ds(2 * pp, 2)]
        pltpu.make_async_copy(both, both, f_recv.at[it, pp]).wait()
        return jnp.concatenate([f_all[it, 2 * pp], f_all[it, 2 * pp + 1]], axis=1)

    def sweep(it):
        image = img[...]
        left = pieces(image)

        def part_of_factor(t, carry):
            pp = near_pair(pairs - 1 - t)
            at = columns(pp)
            part = fold(dot(left, g[:, at]) + dot(left, e[:, at]), rank)
            s_out[it, 2 * pp] = part[:, :piece]
            s_out[it, 2 * pp + 1] = part[:, piece:]
            for k in range(2):

                @pl.when(2 * pp + k != me)
                def _():
                    s_copy(it, 2 * pp + k).start()

            @pl.when(t == 1)
            def _():
                wide = jnp.concatenate([image, jnp.zeros((128 - rank, image.shape[1]), F32)], axis=0)
                gram_in[it, me] = dot_nt(image, wide, precision=lax.Precision.HIGHEST)
                for peer in others()[::-1]:
                    gram_copy(it, peer).start()

            return carry

        lax.fori_loop(0, pairs, part_of_factor, 0)
        from_others(gram_in.at[it], gram_recv.at[it]).wait()
        gram = gram_in[it, 0]
        for p in range(1, n_fsdp):
            gram += gram_in[it, p]
        inv[...] = inverse_cholesky(gram, rank)
        from_others(s_in.at[it], s_recv.at[it]).wait()
        total = s_out[it, me]
        for peer in others():
            total += s_in[it, peer]
        f_own[it] = apply_inverse(inv[...], total, rank)
        for peer in others():
            f_copy(it, peer).start()
        f_local(it).start()

    load_q.wait()

    def first_image(c, image):
        for copy in loads(c):
            copy.wait()
        at = columns(c)
        start = pieces(q[:, at])
        return image + dot_nt(start, g[:, at]) + dot_nt(start, e[:, at])

    zero = jnp.zeros((4 * rank, g.shape[0]), F32)
    img[...] = fold(lax.fori_loop(0, pairs, first_image, zero), rank)
    pl.semaphore_wait(barrier, n_fsdp + n_rep - 2)
    sweep(0)

    def second_image(t, image):
        pp = near_pair(t)
        factor = pieces(f_pair(0, pp))
        at = columns(pp)
        return image + dot_nt(factor, g[:, at]) + dot_nt(factor, e[:, at])

    img[...] = fold(lax.fori_loop(0, pairs, second_image, zero), rank)
    sweep(1)

    def to_replica(src, dst, send, recv, peer):
        return pltpu.make_async_remote_copy(
            src_ref=src, dst_ref=dst, send_sem=send, recv_sem=recv, device_id={"replica": peer}, device_id_type=MESH
        )

    def row_copy(peer):
        return to_replica(z_rows.at[rep], z_rows.at[rep], zr_send, zr_recv, peer)

    def factor_copy(peer):
        return to_replica(f_all.at[1, pl.ds(2 * peer, 2)], z_fac.at[rep], zf_send, zf_recv, peer)

    rows_t = apply_inverse(inv[...], img[...], rank)
    z_rows[rep] = rows_t
    for t in range(1, n_rep):
        row_copy(lax.rem(rep + t, n_rep)).start()
    hi, mid = halves(rows_t)
    left = jnp.concatenate([hi, hi, mid, mid], axis=0).T.astype(BF16)

    def error(t, carry):
        pp = near_pair(t)
        factor = f_pair(1, pp)

        @pl.when(pp != rep)
        def _():
            factor_copy(pp).start()

        hi, mid = halves(factor)
        right = jnp.concatenate([hi, mid, hi, mid], axis=0).astype(BF16)
        at = columns(pp)
        ne_ref[0, :, at] = (g[:, at].astype(F32) + e[:, at].astype(F32) - dot(left, right)).astype(BF16)
        return carry

    lax.fori_loop(0, pairs, error, 0)
    z_fac[rep] = f_all[1, pl.ds(2 * rep, 2)]
    from_others(z_rows, zr_recv).wait()
    from_others(z_fac, zf_recv).wait()

    for it in range(2):
        from_others(gram_in.at[it], gram_send.at[it]).wait()
        from_others(s_out.at[it], s_send.at[it]).wait()
        from_others(f_all.at[it], f_send.at[it]).wait()
    from_others(z_rows, zr_send).wait()
    from_others(z_fac, zf_send).wait()


def finish(ne, z_rows, z_fac, ne_hbm, up_hbm, up, sems):
    n_rep, rank, rows = z_rows.shape
    piece = z_fac.shape[3]
    blocks = sems.shape[0] - 1
    height = rows // blocks
    copies = []
    for b in range(blocks):
        at = pl.ds(b * height, height)
        copies.append(pltpu.make_async_copy(ne.at[0, at], ne_hbm.at[0, at], sems.at[b]))
        copies[-1].start()
    hi, mid = halves(z_rows[...].reshape(n_rep * rank, rows))
    left = jnp.concatenate([hi, hi, mid], axis=0).T.astype(BF16)
    for k in range(2):
        hi, mid = halves(z_fac[:, k].reshape(n_rep * rank, piece))
        right = jnp.concatenate([hi, mid, hi], axis=0).astype(BF16)
        up[:, k * piece : (k + 1) * piece] = (dot(left, right) * (1.0 / n_rep)).astype(BF16)
    copies.append(pltpu.make_async_copy(up, up_hbm, sems.at[blocks]))
    copies[-1].start()
    for copy in copies:
        copy.wait()


def shards(n_rep, n_fsdp, outer_grad, error_prev, q_init):
    rank, cols = q_init.shape
    rows = outer_grad.shape[1]
    piece = cols // n_fsdp
    side = math.isqrt(n_fsdp)
    dma = pltpu.SemaphoreType.DMA
    vmem = pl.BlockSpec(memory_space=pltpu.VMEM)
    hbm = pl.BlockSpec(memory_space=pltpu.HBM)
    parts = pl.pallas_call(
        functools.partial(kernel, n_rep, n_fsdp, side),
        out_shape=[
            pltpu.VMEM((1, rows, cols), BF16),
            pltpu.VMEM((n_rep, rank, rows), F32),
            pltpu.VMEM((n_rep, 2, rank, piece), F32),
        ],
        in_specs=[hbm] * 3,
        out_specs=[vmem] * 3,
        scratch_shapes=[
            pltpu.VMEM((rows, cols), BF16),
            pltpu.VMEM((rows, cols), BF16),
            pltpu.VMEM((rank, cols), F32),
            pltpu.VMEM((rank, rows), F32),
            pltpu.VMEM((rank, 128), F32),
            pltpu.VMEM((2, n_fsdp, rank, 128), F32),
            pltpu.VMEM((2, n_fsdp, rank, piece), F32),
            pltpu.VMEM((2, n_fsdp, rank, piece), F32),
            pltpu.VMEM((2, rank, piece), F32),
            pltpu.VMEM((2, n_fsdp, rank, piece), F32),
            dma((1 + n_fsdp,)),
            dma((2,)),
            dma((2,)),
            dma((2,)),
            dma((2,)),
            dma((2,)),
            dma((2, n_fsdp // 2)),
            dma,
            dma,
            dma,
            dma,
        ],
        compiler_params=pltpu.CompilerParams(
            collective_id=0, has_side_effects=True, vmem_limit_bytes=VMEM_LIMIT
        ),
    )(*(pltpu.with_memory_space_constraint(x, pltpu.HBM) for x in (outer_grad, error_prev, q_init)))
    new_error, update = pl.pallas_call(
        finish,
        out_shape=[pltpu.HBM((1, rows, cols), BF16), pltpu.HBM((rows, cols // n_rep), BF16)],
        in_specs=[vmem] * 3,
        out_specs=[hbm] * 2,
        scratch_shapes=[pltpu.VMEM((rows, cols // n_rep), BF16), dma((9,))],
        compiler_params=pltpu.CompilerParams(vmem_limit_bytes=16 << 20),
    )(*(pltpu.with_memory_space_constraint(x, pltpu.VMEM) for x in parts))
    return update, new_error


VMEM_LIMIT = 40 << 20


def solution(mesh):
    n_rep, n_fsdp = mesh.shape["replica"], mesh.shape["fsdp"]
    return jax.shard_map(
        functools.partial(shards, n_rep, n_fsdp),
        mesh=mesh,
        in_specs=(P("replica", "fsdp", None), P("replica", "fsdp", None), P()),
        out_specs=(P("fsdp", "replica"), P("replica", "fsdp", None)),
        check_vma=False,
    )
```

time: 73.5 us -> 56.7 us (0.77)
  the two profiles are of different devices: /device:TPU:1 before, /device:TPU:17 now
where the time goes in v2:
time: 56.7 us; the launch traced here: 56.1 us
  Pallas kernels  55.5 us (98%)
  between operations  0.64 us (1%)
    pallas_call x1, Pallas kernels, shards(): pl.pallas_call(functools.partial(kernel, n_rep, n_fsdp, side), out_shape=...  52.1 us
    pallas_call x1, Pallas kernels, shards(): pl.pallas_call(finish, out_shape=[pltpu.HBM((1, rows, cols), BF16), pltpu...  3.34 us

profile of v2, /device:TPU:17, one launch (start us, length us, event | category | flops | bytes accessed | tf_op | source)
XLA Modules:
  0.0 56.1 jit_solution(13250793269645761016)
XLA Ops:
  0.6 52.1 %shard_map.50 = (bf16[1,256,14336]{2,1,0:T(8,128)(2,1)S(1)}, f32[8,8,256]{2,1,0:T(8,128)S(1)}, f32[8,2,8,896]{3,2,1,0:T(8,128)S(1)}) custom-call(bf16[1,256,14336]{2,1,0:T(8,128)(2,1)} %g_hbm.1, bf16[1,256,14336]{2,1,0:T(8,128)(2,1)} %e_hbm.1, f32[8,14336]{1,0:T(8,128)} %q_hbm.1), custom_call_target="tpu_custom_call" | custom-call | tf_op jit(solution)/shard_map/pallas_call | solution.py:273
  52.8 3.3 %shard_map.51 = (bf16[1,256,14336]{2,1,0:T(8,128)(2,1)}, bf16[256,1792]{1,0:T(8,128)(2,1)}) custom-call(bf16[1,256,14336]{2,1,0:T(8,128)(2,1)S(1)} %get-tuple-element.7.ne, f32[8,8,256]{2,1,0:T(8,128)S(1)} %get-tuple-element.8.z_rows, f32[8,2,8,896]{3,2,1,0:T(8,128)S(1)} %get-tuple-element.9.z_fac), custom_call_target="tpu_custom_call" | custom-call | tf_op jit(solution)/shard_map/pallas_call | solution.py:309

commit v3 on v2

--- a/solution.py
+++ b/solution.py
@@ -61,7 +61,7 @@
 
 def kernel(
     n_rep, n_fsdp, side, g_hbm, e_hbm, q_hbm, ne_ref, z_rows, z_fac,
-    g, e, q, img, inv, gram_in, s_out, s_in, f_own, f_all,
+    g, e, g_t, e_t, q, img, inv, gram_in, s_out, s_in, f_own, f_all,
     load_sem, gram_send, gram_recv, s_send, s_recv, f_send, f_recv, zr_send, zr_recv, zf_send, zf_recv,
 ):
     rank, cols = q.shape
@@ -136,41 +136,47 @@
         image = img[...]
         left = pieces(image)
 
-        def part_of_factor(t, carry):
-            pp = near_pair(pairs - 1 - t)
-            at = columns(pp)
-            part = fold(dot(left, g[:, at]) + dot(left, e[:, at]), rank)
-            s_out[it, 2 * pp] = part[:, :piece]
-            s_out[it, 2 * pp + 1] = part[:, piece:]
-            for k in range(2):
-
-                @pl.when(2 * pp + k != me)
-                def _():
-                    s_copy(it, 2 * pp + k).start()
-
-            @pl.when(t == 1)
-            def _():
-                wide = jnp.concatenate([image, jnp.zeros((128 - rank, image.shape[1]), F32)], axis=0)
-                gram_in[it, me] = dot_nt(image, wide, precision=lax.Precision.HIGHEST)
-                for peer in others()[::-1]:
-                    gram_copy(it, peer).start()
-
+        def row_at(t):
+            dy = side - 1 - t
+            return lax.rem(my_y + (dy + 1) // 2 * (2 * (dy % 2) - 1) + side, side)
+
+        def row_of_factor(t):
+            first = row_at(t) * side
+            for k in range(side):
+                at = pl.ds(pl.multiple_of((first + k) * piece, piece), piece)
+                s_out[it, first + k] = fold(dot(left, g[:, at]) + dot(left, e[:, at]), rank)
+
+        def send_row(t):
+            for dx in range(side):
+                s_copy(it, row_at(t) * side + lax.rem(my_x + 2 + dx, side)).start()
+
+        def next_row(t, carry):
+            send_row(t - 1)
+            row_of_factor(t)
             return carry
 
-        lax.fori_loop(0, pairs, part_of_factor, 0)
+        row_of_factor(0)
+        wide = jnp.concatenate([left, jnp.zeros((96, left.shape[1]), BF16)], axis=0)
+        terms = fold(dot_nt(left, wide), rank)
+        gram_in[it, me] = terms + pltpu.roll(terms, 128 - rank, 1) + pltpu.roll(terms, 128 - 2 * rank, 1)
+        lax.fori_loop(1, side, next_row, 0)
+        for dx in range(1, side):
+            s_copy(it, my_y * side + lax.rem(my_x + dx, side)).start()
+        for peer in others()[::-1]:
+            gram_copy(it, peer).start()
+        from_others(s_in.at[it], s_recv.at[it]).wait()
+        total = s_out[it, me]
+        for peer in others():
+            total += s_in[it, peer]
+        f_own[it] = total
+        for peer in others():
+            f_copy(it, peer).start()
+        f_local(it).start()
         from_others(gram_in.at[it], gram_recv.at[it]).wait()
         gram = gram_in[it, 0]
         for p in range(1, n_fsdp):
             gram += gram_in[it, p]
         inv[...] = inverse_cholesky(gram, rank)
-        from_others(s_in.at[it], s_recv.at[it]).wait()
-        total = s_out[it, me]
-        for peer in others():
-            total += s_in[it, peer]
-        f_own[it] = apply_inverse(inv[...], total, rank)
-        for peer in others():
-            f_copy(it, peer).start()
-        f_local(it).start()
 
     load_q.wait()
 
@@ -179,7 +185,9 @@
             copy.wait()
         at = columns(c)
         start = pieces(q[:, at])
-        return image + dot_nt(start, g[:, at]) + dot_nt(start, e[:, at])
+        g_t[at, :] = g[:, at].T
+        e_t[at, :] = e[:, at].T
+        return image + dot(start, g_t[at, :]) + dot(start, e_t[at, :])
 
     zero = jnp.zeros((4 * rank, g.shape[0]), F32)
     img[...] = fold(lax.fori_loop(0, pairs, first_image, zero), rank)
@@ -188,9 +196,9 @@
 
     def second_image(t, image):
         pp = near_pair(t)
-        factor = pieces(f_pair(0, pp))
+        factor = pieces(apply_inverse(inv[...], f_pair(0, pp), rank))
         at = columns(pp)
-        return image + dot_nt(factor, g[:, at]) + dot_nt(factor, e[:, at])
+        return image + dot(factor, g_t[at, :]) + dot(factor, e_t[at, :])
 
     img[...] = fold(lax.fori_loop(0, pairs, second_image, zero), rank)
     sweep(1)
@@ -213,20 +221,27 @@
     hi, mid = halves(rows_t)
     left = jnp.concatenate([hi, hi, mid, mid], axis=0).T.astype(BF16)
 
-    def error(t, carry):
+    def forward(t, carry):
         pp = near_pair(t)
-        factor = f_pair(1, pp)
+        factor = apply_inverse(inv[...], f_pair(1, pp), rank)
+        f_all[1, 2 * pp] = factor[:, :piece]
+        f_all[1, 2 * pp + 1] = factor[:, piece:]
 
         @pl.when(pp != rep)
         def _():
             factor_copy(pp).start()
 
-        hi, mid = halves(factor)
+        return carry
+
+    def error(t, carry):
+        pp = near_pair(t)
+        hi, mid = halves(jnp.concatenate([f_all[1, 2 * pp], f_all[1, 2 * pp + 1]], axis=1))
         right = jnp.concatenate([hi, mid, hi, mid], axis=0).astype(BF16)
         at = columns(pp)
         ne_ref[0, :, at] = (g[:, at].astype(F32) + e[:, at].astype(F32) - dot(left, right)).astype(BF16)
         return carry
 
+    lax.fori_loop(0, pairs, forward, 0)
     lax.fori_loop(0, pairs, error, 0)
     z_fac[rep] = f_all[1, pl.ds(2 * rep, 2)]
     from_others(z_rows, zr_recv).wait()
@@ -282,6 +297,8 @@
         scratch_shapes=[
             pltpu.VMEM((rows, cols), BF16),
             pltpu.VMEM((rows, cols), BF16),
+            pltpu.VMEM((cols, rows), BF16),
+            pltpu.VMEM((cols, rows), BF16),
             pltpu.VMEM((rank, cols), F32),
             pltpu.VMEM((rank, rows), F32),
             pltpu.VMEM((rank, 128), F32),
@@ -317,7 +334,7 @@
     return update, new_error
 
 
-VMEM_LIMIT = 40 << 20
+VMEM_LIMIT = 46 << 20
 
 
 def solution(mesh):

time: 56.7 us -> 54.1 us (0.954)
  Pallas kernels: 55.5 us -> 53.4 us
    pallas_call x1, Pallas kernels: 52.1 us -> 50 us  [shards(): pl.pallas_call(functools.partial(kernel, n_rep, n_fsdp, side), out_shape=...]
where the time goes in v3:
time: 54.1 us; the launch traced here: 54 us
  Pallas kernels  53.4 us (99%)
  between operations  0.64 us (1%)
    pallas_call x1, Pallas kernels, shards(): pl.pallas_call(functools.partial(kernel, n_rep, n_fsdp, side), out_shape=...  50 us
    pallas_call x1, Pallas kernels, shards(): pl.pallas_call(finish, out_shape=[pltpu.HBM((1, rows, cols), BF16), pltpu...  3.34 us

profile of v3, /device:TPU:17, one launch (start us, length us, event | category | flops | bytes accessed | tf_op | source)
XLA Modules:
  0.0 54.0 jit_solution(10102057416300953722)
XLA Ops:
  0.6 50.0 %shard_map.50 = (bf16[1,256,14336]{2,1,0:T(8,128)(2,1)S(1)}, f32[8,8,256]{2,1,0:T(8,128)S(1)}, f32[8,2,8,896]{3,2,1,0:T(8,128)S(1)}) custom-call(bf16[1,256,14336]{2,1,0:T(8,128)(2,1)} %g_hbm.1, bf16[1,256,14336]{2,1,0:T(8,128)(2,1)} %e_hbm.1, f32[8,14336]{1,0:T(8,128)} %q_hbm.1), custom_call_target="tpu_custom_call" | custom-call | tf_op jit(solution)/shard_map/pallas_call | solution.py:288
  50.7 3.3 %shard_map.51 = (bf16[1,256,14336]{2,1,0:T(8,128)(2,1)}, bf16[256,1792]{1,0:T(8,128)(2,1)}) custom-call(bf16[1,256,14336]{2,1,0:T(8,128)(2,1)S(1)} %get-tuple-element.7.ne, f32[8,8,256]{2,1,0:T(8,128)S(1)} %get-tuple-element.8.z_rows, f32[8,2,8,896]{3,2,1,0:T(8,128)S(1)} %get-tuple-element.9.z_fac), custom_call_target="tpu_custom_call" | custom-call | tf_op jit(solution)/shard_map/pallas_call | solution.py:326

commit v4 on v3

--- a/solution.py
+++ b/solution.py
@@ -97,14 +97,22 @@
 
     def others():
         steps = [(dy, dx) for dy in range(side) for dx in range(side) if dy or dx]
-        steps.sort(key=lambda s: far(s[0], side) + far(s[1], side))
+        steps.sort(key=lambda s: (far(s[0], side), far(s[1], side)))
         return [lax.rem(my_y + dy, side) * side + lax.rem(my_x + dx, side) for dy, dx in steps]
 
-    def near_pair(t):
+    def over_pairs(step, carry):
         half = side // 2
-        u = t // half
-        dy = (u + 1) // 2 * (2 * (u % 2) - 1) + side
-        return lax.rem(my_y + dy, side) * half + lax.rem(my_x // 2 + t, half)
+
+        def run(rows, count, carry):
+            def at(j, carry):
+                row = lax.rem(my_y + rows(lax.rem(j, count)) + side, side)
+                return step(row * half + lax.rem(my_x // 2 + j // count, half), carry)
+
+            return lax.fori_loop(0, count * half, at, carry)
+
+        carry = run(lambda j: 0 * j, 1, carry)
+        carry = run(lambda j: 1 - 2 * j, 2, carry)
+        return run(lambda j: 2 + j, side - 3, carry)
 
     def to_peer(src, dst, send, recv, peer):
         return pltpu.make_async_remote_copy(
@@ -194,13 +202,12 @@
     pl.semaphore_wait(barrier, n_fsdp + n_rep - 2)
     sweep(0)
 
-    def second_image(t, image):
-        pp = near_pair(t)
+    def second_image(pp, image):
         factor = pieces(apply_inverse(inv[...], f_pair(0, pp), rank))
         at = columns(pp)
         return image + dot(factor, g_t[at, :]) + dot(factor, e_t[at, :])
 
-    img[...] = fold(lax.fori_loop(0, pairs, second_image, zero), rank)
+    img[...] = fold(over_pairs(second_image, zero), rank)
     sweep(1)
 
     def to_replica(src, dst, send, recv, peer):
@@ -221,8 +228,7 @@
     hi, mid = halves(rows_t)
     left = jnp.concatenate([hi, hi, mid, mid], axis=0).T.astype(BF16)
 
-    def forward(t, carry):
-        pp = near_pair(t)
+    def forward(pp, carry):
         factor = apply_inverse(inv[...], f_pair(1, pp), rank)
         f_all[1, 2 * pp] = factor[:, :piece]
         f_all[1, 2 * pp + 1] = factor[:, piece:]
@@ -233,15 +239,14 @@
 
         return carry
 
-    def error(t, carry):
-        pp = near_pair(t)
+    def error(pp, carry):
         hi, mid = halves(jnp.concatenate([f_all[1, 2 * pp], f_all[1, 2 * pp + 1]], axis=1))
         right = jnp.concatenate([hi, mid, hi, mid], axis=0).astype(BF16)
         at = columns(pp)
         ne_ref[0, :, at] = (g[:, at].astype(F32) + e[:, at].astype(F32) - dot(left, right)).astype(BF16)
         return carry
 
-    lax.fori_loop(0, pairs, forward, 0)
+    over_pairs(forward, 0)
     lax.fori_loop(0, pairs, error, 0)
     z_fac[rep] = f_all[1, pl.ds(2 * rep, 2)]
     from_others(z_rows, zr_recv).wait()

time: 54.1 us -> 52.7 us (0.974)
  Pallas kernels: 53.4 us -> 51.9 us
    pallas_call x1, Pallas kernels: 50 us -> 48.6 us  [shards(): pl.pallas_call(functools.partial(kernel, n_rep, n_fsdp, side), out_shape=...]
where the time goes in v4:
time: 52.7 us; the launch traced here: 52.6 us
  Pallas kernels  51.9 us (98%)
  between operations  0.64 us (1%)
    pallas_call x1, Pallas kernels, shards(): pl.pallas_call(functools.partial(kernel, n_rep, n_fsdp, side), out_shape=...  48.6 us
    pallas_call x1, Pallas kernels, shards(): pl.pallas_call(finish, out_shape=[pltpu.HBM((1, rows, cols), BF16), pltpu...  3.34 us

profile of v4, /device:TPU:17, one launch (start us, length us, event | category | flops | bytes accessed | tf_op | source)
XLA Modules:
  0.0 52.6 jit_solution(12073253905010391287)
XLA Ops:
  0.6 48.6 %shard_map.50 = (bf16[1,256,14336]{2,1,0:T(8,128)(2,1)S(1)}, f32[8,8,256]{2,1,0:T(8,128)S(1)}, f32[8,2,8,896]{3,2,1,0:T(8,128)S(1)}) custom-call(bf16[1,256,14336]{2,1,0:T(8,128)(2,1)} %g_hbm.1, bf16[1,256,14336]{2,1,0:T(8,128)(2,1)} %e_hbm.1, f32[8,14336]{1,0:T(8,128)} %q_hbm.1), custom_call_target="tpu_custom_call" | custom-call | tf_op jit(solution)/shard_map/pallas_call | solution.py:293
  49.2 3.3 %shard_map.51 = (bf16[1,256,14336]{2,1,0:T(8,128)(2,1)}, bf16[256,1792]{1,0:T(8,128)(2,1)}) custom-call(bf16[1,256,14336]{2,1,0:T(8,128)(2,1)S(1)} %get-tuple-element.7.ne, f32[8,8,256]{2,1,0:T(8,128)S(1)} %get-tuple-element.8.z_rows, f32[8,2,8,896]{3,2,1,0:T(8,128)S(1)} %get-tuple-element.9.z_fac), custom_call_target="tpu_custom_call" | custom-call | tf_op jit(solution)/shard_map/pallas_call | solution.py:331

commit v5 on v4

--- a/solution.py
+++ b/solution.py
@@ -148,11 +148,13 @@
             dy = side - 1 - t
             return lax.rem(my_y + (dy + 1) // 2 * (2 * (dy % 2) - 1) + side, side)
 
+        def piece_of_factor(p):
+            at = pl.ds(pl.multiple_of(p * piece, piece), piece)
+            s_out[it, p] = fold(dot(left, g[:, at]) + dot(left, e[:, at]), rank)
+
         def row_of_factor(t):
-            first = row_at(t) * side
             for k in range(side):
-                at = pl.ds(pl.multiple_of((first + k) * piece, piece), piece)
-                s_out[it, first + k] = fold(dot(left, g[:, at]) + dot(left, e[:, at]), rank)
+                piece_of_factor(row_at(t) * side + k)
 
         def send_row(t):
             for dx in range(side):
@@ -167,9 +169,16 @@
         wide = jnp.concatenate([left, jnp.zeros((96, left.shape[1]), BF16)], axis=0)
         terms = fold(dot_nt(left, wide), rank)
         gram_in[it, me] = terms + pltpu.roll(terms, 128 - rank, 1) + pltpu.roll(terms, 128 - 2 * rank, 1)
-        lax.fori_loop(1, side, next_row, 0)
-        for dx in range(1, side):
-            s_copy(it, my_y * side + lax.rem(my_x + dx, side)).start()
+        def last_row(j, carry):
+            pl.when(j == 0)(lambda: send_row(side - 2))
+            dx = 2 + j - 3 * (j // 2) - 2 * (j // 3)
+            peer = my_y * side + lax.rem(my_x + dx, side)
+            piece_of_factor(peer)
+            pl.when(peer != me)(lambda: s_copy(it, peer).start())
+            return carry
+
+        lax.fori_loop(1, side - 1, next_row, 0)
+        lax.fori_loop(0, side, last_row, 0)
         for peer in others()[::-1]:
             gram_copy(it, peer).start()
         from_others(s_in.at[it], s_recv.at[it]).wait()
@@ -249,14 +258,14 @@
     over_pairs(forward, 0)
     lax.fori_loop(0, pairs, error, 0)
     z_fac[rep] = f_all[1, pl.ds(2 * rep, 2)]
-    from_others(z_rows, zr_recv).wait()
-    from_others(z_fac, zf_recv).wait()
-
     for it in range(2):
         from_others(gram_in.at[it], gram_send.at[it]).wait()
         from_others(s_out.at[it], s_send.at[it]).wait()
         from_others(f_all.at[it], f_send.at[it]).wait()
     from_others(z_rows, zr_send).wait()
+    from_others(z_rows, zr_recv).wait()
+    from_others(z_fac, zf_recv).wait()
+
     from_others(z_fac, zf_send).wait()
 
 

time: 52.7 us -> 52.4 us (level)
  no operation moved by 1% of the time
where the time goes in v5:
time: 52.4 us; the launch traced here: 52.3 us
  Pallas kernels  51.6 us (98%)
  between operations  0.64 us (1%)
    pallas_call x1, Pallas kernels, shards(): pl.pallas_call(functools.partial(kernel, n_rep, n_fsdp, side), out_shape=...  48.3 us
    pallas_call x1, Pallas kernels, shards(): pl.pallas_call(finish, out_shape=[pltpu.HBM((1, rows, cols), BF16), pltpu...  3.34 us

profile of v5, /device:TPU:17, one launch (start us, length us, event | category | flops | bytes accessed | tf_op | source)
XLA Modules:
  0.0 52.3 jit_solution(11843820197342672315)
XLA Ops:
  0.6 48.3 %shard_map.50 = (bf16[1,256,14336]{2,1,0:T(8,128)(2,1)S(1)}, f32[8,8,256]{2,1,0:T(8,128)S(1)}, f32[8,2,8,896]{3,2,1,0:T(8,128)S(1)}) custom-call(bf16[1,256,14336]{2,1,0:T(8,128)(2,1)} %g_hbm.1, bf16[1,256,14336]{2,1,0:T(8,128)(2,1)} %e_hbm.1, f32[8,14336]{1,0:T(8,128)} %q_hbm.1), custom_call_target="tpu_custom_call" | custom-call | tf_op jit(solution)/shard_map/pallas_call | solution.py:302
  48.9 3.3 %shard_map.51 = (bf16[1,256,14336]{2,1,0:T(8,128)(2,1)}, bf16[256,1792]{1,0:T(8,128)(2,1)}) custom-call(bf16[1,256,14336]{2,1,0:T(8,128)(2,1)S(1)} %get-tuple-element.7.ne, f32[8,8,256]{2,1,0:T(8,128)S(1)} %get-tuple-element.8.z_rows, f32[8,2,8,896]{3,2,1,0:T(8,128)S(1)} %get-tuple-element.9.z_fac), custom_call_target="tpu_custom_call" | custom-call | tf_op jit(solution)/shard_map/pallas_call | solution.py:340

commit v6 on v5

--- a/solution.py
+++ b/solution.py
@@ -87,8 +87,6 @@
             copy.start()
 
     barrier = pltpu.get_barrier_semaphore()
-    for t in range(1, n_fsdp):
-        pl.semaphore_signal(barrier, inc=1, device_id={"fsdp": lax.rem(me + t, n_fsdp)}, device_id_type=MESH)
     for t in range(1, n_rep):
         pl.semaphore_signal(barrier, inc=1, device_id={"replica": lax.rem(rep + t, n_rep)}, device_id_type=MESH)
 
@@ -206,8 +204,17 @@
         e_t[at, :] = e[:, at].T
         return image + dot(start, g_t[at, :]) + dot(start, e_t[at, :])
 
+    share = (n_fsdp - 1) // 3
+
+    def greet_and_image(c, image):
+        for t in range(share):
+            peer = lax.rem(me + 1 + c * share + t, n_fsdp)
+            pl.semaphore_signal(barrier, inc=1, device_id={"fsdp": peer}, device_id_type=MESH)
+        return first_image(c, image)
+
     zero = jnp.zeros((4 * rank, g.shape[0]), F32)
-    img[...] = fold(lax.fori_loop(0, pairs, first_image, zero), rank)
+    image = lax.fori_loop(0, 3, greet_and_image, zero)
+    img[...] = fold(lax.fori_loop(3, pairs, first_image, image), rank)
     pl.semaphore_wait(barrier, n_fsdp + n_rep - 2)
     sweep(0)
 

time: 52.4 us -> 52.5 us (level)
  no operation moved by 1% of the time
where the time goes in v6:
time: 52.5 us; the launch traced here: 52.3 us
  Pallas kernels  51.7 us (98%)
  between operations  0.64 us (1%)
    pallas_call x1, Pallas kernels, shards(): pl.pallas_call(functools.partial(kernel, n_rep, n_fsdp, side), out_shape=...  48.4 us
    pallas_call x1, Pallas kernels, shards(): pl.pallas_call(finish, out_shape=[pltpu.HBM((1, rows, cols), BF16), pltpu...  3.34 us

profile of v6, /device:TPU:17, one launch (start us, length us, event | category | flops | bytes accessed | tf_op | source)
XLA Modules:
  0.0 52.3 jit_solution(18383657599469969252)
XLA Ops:
  0.6 48.4 %shard_map.50 = (bf16[1,256,14336]{2,1,0:T(8,128)(2,1)S(1)}, f32[8,8,256]{2,1,0:T(8,128)S(1)}, f32[8,2,8,896]{3,2,1,0:T(8,128)S(1)}) custom-call(bf16[1,256,14336]{2,1,0:T(8,128)(2,1)} %g_hbm.1, bf16[1,256,14336]{2,1,0:T(8,128)(2,1)} %e_hbm.1, f32[8,14336]{1,0:T(8,128)} %q_hbm.1), custom_call_target="tpu_custom_call" | custom-call | tf_op jit(solution)/shard_map/pallas_call | solution.py:309
  49.0 3.3 %shard_map.51 = (bf16[1,256,14336]{2,1,0:T(8,128)(2,1)}, bf16[256,1792]{1,0:T(8,128)(2,1)}) custom-call(bf16[1,256,14336]{2,1,0:T(8,128)(2,1)S(1)} %get-tuple-element.7.ne, f32[8,8,256]{2,1,0:T(8,128)S(1)} %get-tuple-element.8.z_rows, f32[8,2,8,896]{3,2,1,0:T(8,128)S(1)} %get-tuple-element.9.z_fac), custom_call_target="tpu_custom_call" | custom-call | tf_op jit(solution)/shard_map/pallas_call | solution.py:347
